TPU v7x, 512 devices: a whole 4x4x16 slice. The times are simulated.
512 devices in a mesh: blk: 64 (over y, z_lo, core), tgt: 8 (over x, z_hi).
Axes of the slice: x: 4, y: 4, z: 16 (z_hi: 2, z_lo: 8; z = z_hi * 8 + z_lo), core: 2. Of those that a mesh axis runs over, the one named last changes fastest.
Arguments:
- history: float32 [32768, 1536], P(('blk', 'tgt')), may hold values from 0 to 2
- weights: bfloat16 [64, 512, 32768], P(None, 'tgt', 'blk'), may hold values from -0.03125 to 0.03125
- delays: int32 [32, 32], replicated, may hold values from 16 to 64
- area_blocks: int32 [32], replicated, may hold values from 1 to 3, 64 in all
- potential: float32 [24, 32768], P(None, ('blk', 'tgt')), may hold values from -6 to 6
- leak: float32 [32768], P(('blk', 'tgt')), may hold values from 0.03 to 0.6
- drive: float32 [32768], P(('blk', 'tgt')), may hold values from -6 to 6
Outputs:
- rate_steps: float32 [16, 24, 32768], P(None, None, ('blk', 'tgt'))
- last_potential: float32 [24, 32768], P(None, ('blk', 'tgt'))
Inputs may be any that keep to these rules, and one draw needn't show every extreme that they name: Area a consists of area_blocks[a] consecutive blocks of 512 neurons; areas follow one another in order.
All inputs are finite; a program needn't handle non-finite values.
Results may differ from a plain program's by a relative error of at most 0.00083.
Values may be sent and summed in bfloat16 or wider, within the bound.
A program may use at most 128 MiB of HBM per device.

v0:
```python
import jax
import jax.numpy as jnp
from jax import lax
from jax.sharding import PartitionSpec as P

STEPS = 16


def cut_along(x, dim, peers):
    lengths = x.shape
    parts = x.reshape(*lengths[:dim], peers, lengths[dim] // peers, *lengths[dim + 1 :])
    return jnp.moveaxis(parts, dim, 0)


def summed_on_arrival(x, axis, dim):
    parts = cut_along(x, dim, lax.axis_size(axis))
    arrived = lax.all_to_all(parts, axis, split_axis=0, concat_axis=0, tiled=True)
    return arrived.sum(axis=0)


def block_areas(area_blocks, block_count):
    boundary = jnp.cumsum(area_blocks)
    blocks = jnp.arange(block_count, dtype=jnp.int32)
    return jnp.sum((boundary[None, :] <= blocks[:, None]).astype(jnp.int32), axis=1)


def on_device(history, weights, delays, area_blocks, potential, leak, drive):
    block_count = weights.shape[0]
    piece_width = weights.shape[1]
    columns = history.shape[1]
    trial_count = potential.shape[0]
    window_width = STEPS * trial_count
    area_of_block = block_areas(area_blocks, block_count)
    my_block = lax.axis_index("blk")
    my_area = area_of_block[my_block]
    history_low = history.astype(jnp.bfloat16)

    def window(lag_step, column):
        start = columns - lag_step * trial_count
        return lax.dynamic_slice_in_dim(column, start, window_width, 1)

    lag_steps = delays[my_area][area_of_block]
    arrived = lax.all_gather(history_low, "blk", axis=0, tiled=True)
    shard_count = arrived.shape[0] // piece_width
    shaped = arrived.reshape(shard_count, piece_width, columns)
    delayed_input = jax.vmap(window, in_axes=(0, 0))(lag_steps, shaped)
    partial_input = jnp.einsum(
        "gyw,gyt->wt", delayed_input, weights, preferred_element_type=jnp.float32
    )
    own_input = summed_on_arrival(partial_input, "tgt", 1)
    own_input = own_input.reshape(STEPS, trial_count, piece_width)

    def advance(membrane_state, synaptic):
        membrane_state = membrane_state + leak * (drive - membrane_state + synaptic)
        return (membrane_state, jax.nn.softplus(membrane_state))

    last_potential, rate_steps = lax.scan(advance, potential, own_input)
    return (rate_steps, last_potential)


def solution(mesh):
    in_specs = (
        P(("blk", "tgt"), None),
        P(None, "tgt", "blk"),
        P(),
        P(),
        P(None, ("blk", "tgt")),
        P(("blk", "tgt")),
        P(("blk", "tgt")),
    )
    out_specs = (P(None, None, ("blk", "tgt")), P(None, ("blk", "tgt")))
    return jax.shard_map(
        on_device, mesh=mesh, in_specs=in_specs, out_specs=out_specs, check_vma=False
    )
```

profile of v0, /device:TPU:32, one launch (start us, length us, event | category | flops | bytes accessed | tf_op | source)
XLA Modules:
  0.0 295.5 jit_solution(2415706052495670528)
XLA Ops:
  7.2 0.0 copy-start
  7.2 0.0 all-gather.2.cloned.1.call-start
  7.2 1.7 convert_element_type.6
  8.9 0.0 all-gather.2.cloned.1.call-update
  8.9 0.7 copy.26
  9.7 0.1 reduce-window.8
  9.7 0.1 reduce
  9.9 0.1 convert_reduce_fusion
  10.0 0.6 dynamic_slice.10
  12.2 0.0 copy-done
  12.3 0.8 gather_fusion
  13.1 135.9 %all-gather.2.cloned.1.call-done = bf16[4096,1536]{1,0:T(8,128)(2,1)} async-done(((bf16[64,1536]{1,0:T(8,128)(2,1)}), bf16[4096,1536]{1,0:T(8,128)(2,1)}) %all-gather.2.cloned.1.call-update) | async-done | bytes 12582928 | tf_op jit(solution)/shard_map/all_gather | solution.py:43
  149.0 35.0 %copy.27 = bf16[64,64,1536]{1,0,2:T(8,128)(2,1)} copy(bf16[64,64,1536]{2,1,0:T(8,128)(2,1)} %bitcast.39) | data formatting | bytes 25165824 | tf_op jit(solution)/shard_map/reshape | solution.py:45
  184.0 24.2 %gather_fusion.1 = bf16[64,64,384]{1,0,2:T(8,128)(2,1)} fusion(bf16[64,64,1536]{1,0,2:T(8,128)(2,1)} %copy.27, s32[64]{0:T(128)S(1)} %or_bitcast_fusion), kind=kCustom, calls=%fused_computation.1 | custom fusion | bytes 6292224 | tf_op jit(solution)/shard_map/vmap()/gather | solution.py:40
  208.1 0.0 copy-start.2
  208.2 0.0 copy-start.3
  208.2 0.0 copy-start.4
  208.2 12.3 %fusion.4 = f32[384,512,1]{0,1,2:T(8,128)} fusion(bf16[64,64,512]{2,1,0:T(8,128)(2,1)} %param.10, bf16[64,64,384]{1,0,2:T(8,128)(2,1)} %gather_fusion.1), kind=kOutput, calls=%fused_computation.8 | convolution fusion | flops 1610612736 | bytes 8126464 | tf_op jit(solution)/shard_map/gyw,gyt->wt/dot_general | solution.py:47
  220.5 10.0 %all-to-all-start = ((f32[8,384,64]{1,2,0:T(8,128)}), f32[8,384,64]{1,2,0:T(8,128)S(1)}, u32[]{:S(2)}, u32[]{:S(2)}) async-start(f32[8,384,64]{1,2,0:T(8,128)} %bitcast.13), calls=%async_computation | async-start | bytes 1572864 | tf_op jit(solution)/shard_map/all_to_all | solution.py:17
  230.5 47.3 %all-to-all-done = f32[8,384,64]{1,2,0:T(8,128)S(1)} async-done(((f32[8,384,64]{1,2,0:T(8,128)}), f32[8,384,64]{1,2,0:T(8,128)S(1)}, u32[]{:S(2)}, u32[]{:S(2)}) %all-to-all-start) | async-done | bytes 786464 | tf_op jit(solution)/shard_map/all_to_all | solution.py:17
  277.9 0.1 copy.30
  278.0 0.0 copy-done.2
  278.0 0.0 copy-done.3
  278.1 0.0 copy-done.4
  278.1 10.0 %while.12 = (s32[]{:T(128)}, f32[24,64]{1,0:T(8,128)S(1)}, f32[16,24,64]{2,1,0:T(8,128)}, f32[64]{0:T(128)S(1)}, f32[64]{0:T(128)S(1)}, /*index=5*/f32[16,24,64]{2,1,0:T(8,128)S(1)}, s32[]{:T(128)}) while((s32[]{:T(128)}, f32[24,64]{1,0:T(8,128)S(1)}, f32[16,24,64]{2,1,0:T(8,128)}, f32[64]{0:T(128)S(1)}, f32[64]{0:T(128)S(1)}, ...), condition=%wide.region_4.5_spmd, body=%wide.region_3.4_spmd.sunk | while | flops 15362 | bytes 31821 | solution.py:57
  278.1 0.6 fusion.11
  278.7 0.6 fusion.11
  279.3 0.6 fusion.11
  280.0 0.6 fusion.11
  280.6 0.6 fusion.11
  281.2 0.6 fusion.11
  281.8 0.6 fusion.11
  282.5 0.6 fusion.11
  283.1 0.6 fusion.11
  283.7 0.6 fusion.11
  284.3 0.6 fusion.11
  285.0 0.6 fusion.11
  285.6 0.6 fusion.11
  286.2 0.6 fusion.11
  286.8 0.6 fusion.11
  287.4 0.6 fusion.11
  288.1 0.0 copy-start.1
  288.1 0.6 copy-done.1
  (6 shorter events, 0.1 us)
Async XLA Ops:
  7.2 5.1 %copy-start = (s32[32,32]{1,0:T(8,128)S(1)}, s32[32,32]{1,0:T(8,128)}, u32[]{:S(2)}) copy-start(s32[32,32]{1,0:T(8,128)} %param.11) | copy-start | bytes 12292
  7.2 141.8 %all-gather.2.cloned.1.call-start = ((), (), s32[]{:S(2)}) async-start(), calls=%async_computation.1 | async-start | bytes 12779520 | tf_op jit(solution)/shard_map/all_gather | solution.py:43
  208.1 69.9 %copy-start.2 = (f32[24,64]{1,0:T(8,128)S(1)}, f32[24,64]{1,0:T(8,128)}, u32[]{:S(2)}) copy-start(f32[24,64]{1,0:T(8,128)} %param.13) | copy-start | bytes 18436
  208.2 69.9 %copy-start.3 = (f32[64]{0:T(128)S(1)}, f32[64]{0:T(128)}, u32[]{:S(2)}) copy-start(f32[64]{0:T(128)} %param.14) | copy-start | bytes 772
  208.2 69.9 %copy-start.4 = (f32[64]{0:T(128)S(1)}, f32[64]{0:T(128)}, u32[]{:S(2)}) copy-start(f32[64]{0:T(128)} %param.15) | copy-start | bytes 772
  220.5 57.4 %all-to-all-start = ((f32[8,384,64]{1,2,0:T(8,128)}), f32[8,384,64]{1,2,0:T(8,128)S(1)}, u32[]{:S(2)}, u32[]{:S(2)}) async-start(f32[8,384,64]{1,2,0:T(8,128)} %bitcast.13), calls=%async_computation | async-start | bytes 1572864 | tf_op jit(solution)/shard_map/all_to_all | solution.py:17
  288.1 0.6 copy-start.1
Sparse Core Ops, SparseCore 0:
  10.7 138.2 all-gather.1
where the time goes:
time: 297 us; the launch traced here: 296 us
  waiting for transfers between devices  183 us (62%)
  local copies, waits for them, and re-layouts  62 us (21%)
  between operations  15.8 us (5%)
  matrix products  12.3 us (4%)
  other arithmetic  12 us (4%)
  starting transfers between devices  10.1 us (3%)
    all_gather x1, waiting for transfers between devices, on_device(): arrived = lax.all_gather(history_low, 'blk', axis=0, tiled=True)  136 us
    all_to_all x1, waiting for transfers between devices, summed_on_arrival(): lax.all_to_all(parts, axis, split_axis=0, concat_axis=0, tiled=True)  47.3 us
    reshape x1, local copies, waits for them, and re-layouts, on_device(): shaped = arrived.reshape(shard_count, piece_width, columns)  35 us
    gather x1, local copies, waits for them, and re-layouts, window(): return lax.dynamic_slice_in_dim(column, start, window_width, 1)  24.2 us
    dot_general x1, matrix products, on_device(): jnp.einsum('gyw,gyt->wt', delayed_input, weights, preferred_element_type=...  12.3 us
    all_to_all x1, starting transfers between devices, summed_on_arrival(): lax.all_to_all(parts, axis, split_axis=0, concat_axis=0, tiled=True)  10 us
    dynamic_update_slice x16, other arithmetic, on_device(): last_potential, rate_steps = lax.scan(advance, potential, own_input)  9.98 us
  transfers between devices with their start and end apart: 2, of which 2 were waited for; matrix products, arithmetic and copies ran while one was open for 1% of the time, Pallas kernels for 0%

commit v1 on v0

--- a/solution.py
+++ b/solution.py
@@ -40,7 +40,9 @@
         return lax.dynamic_slice_in_dim(column, start, window_width, 1)
 
     lag_steps = delays[my_area][area_of_block]
-    arrived = lax.all_gather(history_low, "blk", axis=0, tiled=True)
+    arrived = jnp.concatenate(
+        jax.lax.all_to_all(jnp.stack([history_low] * jax.lax.axis_size("blk")), "blk", 0, 0), axis=0
+    )
     shard_count = arrived.shape[0] // piece_width
     shaped = arrived.reshape(shard_count, piece_width, columns)
     delayed_input = jax.vmap(window, in_axes=(0, 0))(lag_steps, shaped)

time: 297 us -> 697 us (2.35)
  the two profiles are of different devices: /device:TPU:32 before, /device:TPU:19 now
where the time goes in v1:
time: 697 us; the launch traced here: 696 us
  waiting for transfers between devices  575 us (82%)
  local copies, waits for them, and re-layouts  67.4 us (10%)
  starting transfers between devices  26.8 us (4%)
  matrix products  12.4 us (2%)
  other arithmetic  11.3 us (2%)
    all_to_all x1, waiting for transfers between devices, on_device(): jax.lax.all_to_all(jnp.stack([history_low] * jax.lax.axis_size('blk')), '...  542 us
    all_to_all x1, local copies, waits for them, and re-layouts, on_device(): jax.lax.all_to_all(jnp.stack([history_low] * jax.lax.axis_size('blk')), '...  35 us
    all_to_all x1, waiting for transfers between devices, summed_on_arrival(): lax.all_to_all(parts, axis, split_axis=0, concat_axis=0, tiled=True)  32.9 us
    gather x1, local copies, waits for them, and re-layouts, window(): return lax.dynamic_slice_in_dim(column, start, window_width, 1)  24.2 us
    all_to_all x1, starting transfers between devices, on_device(): jax.lax.all_to_all(jnp.stack([history_low] * jax.lax.axis_size('blk')), '...  16.8 us
  transfers between devices with their start and end apart: 2, of which 2 were waited for; matrix products, arithmetic and copies ran while one was open for 0% of the time, Pallas kernels for 0%

profile of v1, /device:TPU:19, one launch (start us, length us, event | category | flops | bytes accessed | tf_op | source)
XLA Modules:
  0.0 695.6 jit_solution(12048705581603764835)
XLA Ops:
  0.6 0.0 copy-start
  0.6 1.0 convert_element_type.6
  1.7 6.1 stack.2
  7.8 0.0 copy-start.5
  7.8 16.8 %all-to-all-start = ((bf16[64,64,1536]{2,1,0:T(8,128)(2,1)}), bf16[64,64,1536]{2,1,0:T(8,128)(2,1)}, u32[]{:S(2)}, u32[]{:S(2)}) async-start(bf16[64,64,1536]{2,1,0:T(8,128)(2,1)} %stack.2), calls=%async_computation | async-start | bytes 25165824 | tf_op jit(solution)/shard_map/all_to_all | solution.py:44
  24.5 0.0 copy-done.5
  24.5 0.1 copy.26
  24.6 0.1 reduce-window.8
  24.7 0.1 reduce
  24.8 0.1 convert_reduce_fusion
  24.9 0.6 dynamic_slice.10
  27.4 0.0 copy-done
  27.5 0.8 gather_fusion
  28.3 542.0 %all-to-all-done = bf16[64,64,1536]{2,1,0:T(8,128)(2,1)} async-done(((bf16[64,64,1536]{2,1,0:T(8,128)(2,1)}), bf16[64,64,1536]{2,1,0:T(8,128)(2,1)}, u32[]{:S(2)}, u32[]{:S(2)}) %all-to-all-start) | async-done | bytes 12582944 | tf_op jit(solution)/shard_map/all_to_all | solution.py:44
  570.3 35.0 %copy.27 = bf16[64,64,1536]{1,0,2:T(8,128)(2,1)} copy(bf16[64,64,1536]{2,1,0:T(8,128)(2,1)} %all-to-all-done) | data formatting | bytes 25165824 | tf_op jit(solution)/shard_map/all_to_all | solution.py:44
  605.3 24.2 %gather_fusion.1 = bf16[64,64,384]{1,0,2:T(8,128)(2,1)} fusion(bf16[64,64,1536]{1,0,2:T(8,128)(2,1)} %copy.27, s32[64]{0:T(128)S(1)} %or_bitcast_fusion), kind=kCustom, calls=%fused_computation.1 | custom fusion | bytes 6292224 | tf_op jit(solution)/shard_map/vmap()/gather | solution.py:40
  629.5 0.0 copy-start.2
  629.5 0.0 copy-start.3
  629.5 0.0 copy-start.4
  629.5 12.4 %fusion.4 = f32[384,512,1]{0,1,2:T(8,128)} fusion(bf16[64,64,512]{2,1,0:T(8,128)(2,1)} %param.10, bf16[64,64,384]{1,0,2:T(8,128)(2,1)} %gather_fusion.1), kind=kOutput, calls=%fused_computation.8 | convolution fusion | flops 1610612736 | bytes 8126464 | tf_op jit(solution)/shard_map/gyw,gyt->wt/dot_general | solution.py:49
  641.9 10.0 %all-to-all-start.1 = ((f32[8,384,64]{1,2,0:T(8,128)}), f32[8,384,64]{1,2,0:T(8,128)S(1)}, u32[]{:S(2)}, u32[]{:S(2)}) async-start(f32[8,384,64]{1,2,0:T(8,128)} %bitcast.12), calls=%async_computation.1 | async-start | bytes 1572864 | tf_op jit(solution)/shard_map/all_to_all | solution.py:17
  651.9 32.9 %all-to-all-done.1 = f32[8,384,64]{1,2,0:T(8,128)S(1)} async-done(((f32[8,384,64]{1,2,0:T(8,128)}), f32[8,384,64]{1,2,0:T(8,128)S(1)}, u32[]{:S(2)}, u32[]{:S(2)}) %all-to-all-start.1) | async-done | bytes 786464 | tf_op jit(solution)/shard_map/all_to_all | solution.py:17
  684.8 0.1 copy.30
  684.9 0.0 copy-done.2
  684.9 0.0 copy-done.3
  685.0 0.0 copy-done.4
  685.0 10.0 %while.12 = (s32[]{:T(128)}, f32[24,64]{1,0:T(8,128)S(1)}, f32[16,24,64]{2,1,0:T(8,128)}, f32[64]{0:T(128)S(1)}, f32[64]{0:T(128)S(1)}, /*index=5*/f32[16,24,64]{2,1,0:T(8,128)S(1)}, s32[]{:T(128)}) while((s32[]{:T(128)}, f32[24,64]{1,0:T(8,128)S(1)}, f32[16,24,64]{2,1,0:T(8,128)}, f32[64]{0:T(128)S(1)}, f32[64]{0:T(128)S(1)}, ...), condition=%wide.region_4.5_spmd, body=%wide.region_3.4_spmd.sunk | while | flops 15362 | bytes 31821 | solution.py:59
  685.0 0.6 fusion.11
  685.6 0.6 fusion.11
  686.2 0.6 fusion.11
  686.9 0.6 fusion.11
  687.5 0.6 fusion.11
  688.1 0.6 fusion.11
  688.7 0.6 fusion.11
  689.4 0.6 fusion.11
  690.0 0.6 fusion.11
  690.6 0.6 fusion.11
  691.2 0.6 fusion.11
  691.8 0.6 fusion.11
  692.5 0.6 fusion.11
  693.1 0.6 fusion.11
  693.7 0.6 fusion.11
  694.3 0.6 fusion.11
  695.0 0.0 copy-start.1
  695.0 0.6 copy-done.1
  (6 shorter events, 0.1 us)
Async XLA Ops:
  0.6 26.8 %copy-start = (s32[32,32]{1,0:T(8,128)S(1)}, s32[32,32]{1,0:T(8,128)}, u32[]{:S(2)}) copy-start(s32[32,32]{1,0:T(8,128)} %param.11) | copy-start | bytes 12292
  7.8 16.8 %copy-start.5 = (s32[32]{0:T(128)S(1)}, s32[32]{0:T(128)}, u32[]{:S(2)}) copy-start(s32[32]{0:T(128)} %param.12) | copy-start | bytes 388
  7.8 562.6 %all-to-all-start = ((bf16[64,64,1536]{2,1,0:T(8,128)(2,1)}), bf16[64,64,1536]{2,1,0:T(8,128)(2,1)}, u32[]{:S(2)}, u32[]{:S(2)}) async-start(bf16[64,64,1536]{2,1,0:T(8,128)(2,1)} %stack.2), calls=%async_computation | async-start | bytes 25165824 | tf_op jit(solution)/shard_map/all_to_all | solution.py:44
  629.5 55.5 %copy-start.2 = (f32[24,64]{1,0:T(8,128)S(1)}, f32[24,64]{1,0:T(8,128)}, u32[]{:S(2)}) copy-start(f32[24,64]{1,0:T(8,128)} %param.13) | copy-start | bytes 18436
  629.5 55.5 %copy-start.3 = (f32[64]{0:T(128)S(1)}, f32[64]{0:T(128)}, u32[]{:S(2)}) copy-start(f32[64]{0:T(128)} %param.14) | copy-start | bytes 772
  629.5 55.5 %copy-start.4 = (f32[64]{0:T(128)S(1)}, f32[64]{0:T(128)}, u32[]{:S(2)}) copy-start(f32[64]{0:T(128)} %param.15) | copy-start | bytes 772
  641.9 42.9 %all-to-all-start.1 = ((f32[8,384,64]{1,2,0:T(8,128)}), f32[8,384,64]{1,2,0:T(8,128)S(1)}, u32[]{:S(2)}, u32[]{:S(2)}) async-start(f32[8,384,64]{1,2,0:T(8,128)} %bitcast.12), calls=%async_computation.1 | async-start | bytes 1572864 | tf_op jit(solution)/shard_map/all_to_all | solution.py:17
  695.0 0.6 copy-start.1
